TPU v7x, 32 devices: a whole 2x2x4 slice. The times are simulated.
32 devices in a mesh: batch: 8 (over z, y), seq: 4 (over x, core).
Axes of the slice: x: 2, y: 2, z: 4, core: 2. Of those that a mesh axis runs over, the one named last changes fastest.
Arguments:
- inputs: bfloat16 [24, 1024, 512], P('batch', 'seq'), may hold values from -6 to 6
- counts: int32 [24], P('batch'), may hold values from 128 to 1024, as said below
- cotangent: bfloat16 [24, 1024, 512], P('batch', 'seq'), may hold values from -6 to 6
- attention_weights: float32 [4, 512, 512], P('seq', None, 'batch')
- attention_momenta: float32 [4, 512, 512], P('seq', None, 'batch')
- feed_weights: float32 [2, 512, 2048], P(None, None, ('batch', 'seq'))
- feed_momenta: float32 [2, 512, 2048], P(None, None, ('batch', 'seq'))
- vector_params: float32 [12, 512], P('seq', 'batch')
- vector_first: float32 [12, 512], P('seq', 'batch')
- vector_second: float32 [12, 512], P('seq', 'batch')
Outputs:
- layer_out: bfloat16 [24, 1024, 512], P('batch', 'seq')
- input_grad: bfloat16 [24, 1024, 512], P('batch', 'seq')
- attention_next: float32 [4, 512, 512], P('seq', None, 'batch')
- attention_moment: float32 [4, 512, 512], P('seq', None, 'batch')
- feed_next: float32 [2, 512, 2048], P(None, None, ('batch', 'seq'))
- feed_moment: float32 [2, 512, 2048], P(None, None, ('batch', 'seq'))
- vector_next: float32 [12, 512], P('seq', 'batch')
- vector_first_next: float32 [12, 512], P('seq', 'batch')
- vector_second_next: float32 [12, 512], P('seq', 'batch')
Inputs may be any that keep to these rules, and one draw needn't show every extreme that they name: `counts`: in each aligned block of 3 sequences, one sequence has true tokens in the upper half of the slots of the last index of seq; some sequence has exactly 1024.
All inputs are finite; a program needn't handle non-finite values.
Results may differ from a plain program's by a relative error of at most 0.014.
Values may be sent and summed in bfloat16 or wider, within the bound.
No kernel may reach another device: no remote copies, remote signals or barrier semaphores. Data moves between devices by JAX's collectives and lax.ppermute only.
A program may use at most 128 MiB of HBM per device.

v0:
```python
import jax
import jax.numpy as jnp
from jax import lax
from jax.sharding import PartitionSpec as P

HEAD_DIM = 64
STEP = 10
NS_STEPS = 5


newton_coef = (3.4445, -4.775, 2.0315)
muon_rate = 0.6
muon_decay = 0.95
adam_rate = 0.3
beta_one = 0.9
beta_two = 0.999
decay_rate = 0.01
adam_eps = 1e-08
norm_eps = 1e-05
masked_score = -1e30
highest = lax.Precision.HIGHEST
contract_rows = (((0,), (0,)), ((), ()))
contract_cols = (((1,), (1,)), ((), ()))


def layer_norm(values_in, gain_vec, shift_vec):
    centre = values_in - jnp.mean(values_in, axis=-1, keepdims=True)
    inverse_dev = lax.rsqrt(jnp.mean(centre * centre, axis=-1, keepdims=True) + norm_eps)
    return centre * inverse_dev * gain_vec + shift_vec


def smooth_gate(values_in):
    return jax.nn.gelu(values_in, approximate=True)


def masked_scores(query_rows, key_rows, length, key_span):
    raw_scores = jnp.einsum(
        "qhd,khd->hqk", query_rows, key_rows, preferred_element_type=jnp.float32
    )
    raw_scores = raw_scores * query_rows.shape[2] ** (-0.5)
    live_keys = jnp.arange(key_span) < length
    return jnp.where(live_keys[None, None, :], raw_scores, masked_score)


def attend_span(query_rows, key_rows, value_rows, length, key_span):
    scores = masked_scores(query_rows, key_rows, length, key_span)
    highest_score = jnp.max(scores, axis=2, keepdims=True)
    exponents = jnp.exp(scores - highest_score)
    total_mass = jnp.sum(exponents, axis=2, keepdims=True)
    weights_low = (exponents / total_mass).astype(jnp.bfloat16)
    mixed = jnp.einsum("hqk,khd->qhd", weights_low, value_rows, preferred_element_type=jnp.float32)
    log_mass = (highest_score + jnp.log(total_mass))[:, :, 0]
    return (mixed.astype(jnp.bfloat16), log_mass)


def attend_back_span(query_rows, key_rows, value_rows, grad_mixed, log_mass, length, key_span):
    scores = masked_scores(query_rows, key_rows, length, key_span)
    weights = jnp.exp(scores - log_mass[:, :, None])
    grad_weights = jnp.einsum(
        "qhd,khd->hqk", grad_mixed, value_rows, preferred_element_type=jnp.float32
    )
    inner_sum = jnp.sum(weights * grad_weights, axis=2, keepdims=True)
    grad_scores = (weights * (grad_weights - inner_sum)).astype(jnp.bfloat16)
    score_scale = query_rows.shape[2] ** (-0.5)
    grad_query = (
        jnp.einsum("hqk,khd->qhd", grad_scores, key_rows, preferred_element_type=jnp.float32)
        * score_scale
    )
    grad_key = (
        jnp.einsum("hqk,qhd->khd", grad_scores, query_rows, preferred_element_type=jnp.float32)
        * score_scale
    )
    grad_value = jnp.einsum(
        "hqk,qhd->khd", weights.astype(jnp.bfloat16), grad_mixed, preferred_element_type=jnp.float32
    )
    padding = ((0, key_rows.shape[0] - key_span), (0, 0), (0, 0))
    return (
        grad_query.astype(jnp.bfloat16),
        grad_key.astype(jnp.bfloat16),
        grad_value.astype(jnp.bfloat16),
    )


def gram_of(matrix_part):
    return jnp.einsum("mdc,mec->mde", matrix_part, matrix_part, precision=highest)


def gram_sums(part_att, part_feed):
    gram_att = lax.psum(gram_of(part_att), "batch")
    gram_feed = lax.psum(gram_of(part_feed), ("batch", "seq"))
    return (gram_att, gram_feed)


def start_iterate(matrix_part, gram_whole):
    trace_value = jnp.trace(gram_whole, axis1=1, axis2=2)
    factor = 1.0 / (jnp.sqrt(trace_value) + 1e-07)
    return (matrix_part * factor[:, None, None], gram_whole * (factor * factor)[:, None, None])


def newton_turn(matrix_part, square):
    applied_once = jnp.einsum("mde,mec->mdc", square, matrix_part, precision=highest)
    applied_twice = jnp.einsum("mde,mec->mdc", square, applied_once, precision=highest)
    return (
        newton_coef[0] * matrix_part
        + newton_coef[1] * applied_once
        + newton_coef[2] * applied_twice
    )


def shards(
    inputs,
    counts,
    cotangent,
    attention_weights,
    attention_momenta,
    feed_weights,
    feed_momenta,
    vector_params,
    vector_first,
    vector_second,
):
    seqs_local, local_len, width = inputs.shape
    seq_count = lax.axis_size("seq")
    batch_count = lax.axis_size("batch")
    attention_local = attention_weights.shape[0]
    column_width = attention_weights.shape[2]
    feed_width = feed_weights.shape[2]
    vector_rows = vector_params.shape[0]
    att_low = attention_weights.astype(jnp.bfloat16).reshape(
        attention_local, width, 1, column_width
    )
    feed_low = feed_weights.astype(jnp.bfloat16).reshape(2, width, 1, 1, feed_width)
    vec_low = vector_params.astype(jnp.bfloat16).reshape(vector_rows, 1, column_width)
    att_low, feed_low, vec_low = (
        lax.all_gather(att_low, "seq", axis=0, tiled=True),
        lax.all_gather(feed_low, "seq", axis=3, tiled=True),
        lax.all_gather(vec_low, "seq", axis=0, tiled=True),
    )
    att_low, feed_low, vec_low = (
        lax.all_gather(att_low, "batch", axis=2, tiled=True),
        lax.all_gather(feed_low, "batch", axis=2, tiled=True),
        lax.all_gather(vec_low, "batch", axis=1, tiled=True),
    )
    att_full = att_low.reshape(4, width, width)
    hidden_width = feed_low.shape[2] * feed_low.shape[3] * feed_width
    feed_full = feed_low.reshape(2, width, hidden_width)
    vec_full = vec_low.reshape(12, width).astype(jnp.float32)
    w_query = att_full[0]
    w_key = att_full[1]
    w_value = att_full[2]
    w_output = att_full[3]
    w_up = feed_full[0]
    w_down = feed_full[1]
    bias_query = vec_full[0]
    bias_value = vec_full[1]
    bias_output = vec_full[2]
    bias_up = vec_full[3:7].reshape(hidden_width)
    bias_down = vec_full[7]
    gain_first = vec_full[8]
    shift_first = vec_full[9]
    gain_second = vec_full[10]
    shift_second = vec_full[11]
    tokens = inputs.reshape(seqs_local * local_len, width)

    def project(weight):
        return jnp.dot(tokens, weight, preferred_element_type=jnp.float32)

    def shaped(values_in):
        return values_in.reshape(seqs_local, local_len, width)

    query_tok = (project(w_query) + bias_query).astype(jnp.bfloat16)
    key_tok = project(w_key).astype(jnp.bfloat16)
    value_tok = (project(w_value) + bias_value).astype(jnp.bfloat16)
    heads_query, heads_key, heads_value = (
        lax.all_to_all(shaped(query_tok), "seq", split_axis=2, concat_axis=1, tiled=True),
        lax.all_to_all(shaped(key_tok), "seq", split_axis=2, concat_axis=1, tiled=True),
        lax.all_to_all(shaped(value_tok), "seq", split_axis=2, concat_axis=1, tiled=True),
    )
    full_len = heads_query.shape[1]
    head_width = heads_query.shape[2]
    head_count = head_width // HEAD_DIM
    split_shape = (seqs_local, full_len, head_count, HEAD_DIM)

    def attend_one(packed):
        query_rows, key_rows, value_rows, length = packed
        return attend_span(query_rows, key_rows, value_rows, length, full_len)

    mixed_heads, log_mass = lax.map(
        attend_one,
        (
            heads_query.reshape(split_shape),
            heads_key.reshape(split_shape),
            heads_value.reshape(split_shape),
            counts,
        ),
    )
    mixed_tok = lax.all_to_all(
        mixed_heads.reshape(seqs_local, full_len, head_width),
        "seq",
        split_axis=1,
        concat_axis=2,
        tiled=True,
    )
    mixed_flat = mixed_tok.reshape(-1, width)
    attn_out = jnp.dot(mixed_flat, w_output, preferred_element_type=jnp.float32) + bias_output
    first_in = tokens.astype(jnp.float32) + attn_out
    normed, norm_first_back = jax.vjp(layer_norm, first_in, gain_first, shift_first)
    normed_low = normed.astype(jnp.bfloat16)
    up_pre = jnp.dot(normed_low, w_up, preferred_element_type=jnp.float32) + bias_up
    activated, gate_back = jax.vjp(smooth_gate, up_pre)
    activated_low = activated.astype(jnp.bfloat16)
    down_out = (
        lax.dot_general(activated_low, w_down, contract_cols, preferred_element_type=jnp.float32)
        + bias_down
    )
    summed = tokens.astype(jnp.float32) + normed + down_out
    result, norm_second_back = jax.vjp(layer_norm, summed, gain_second, shift_second)
    layer_out = result.astype(jnp.bfloat16).reshape(inputs.shape)
    grad_out = cotangent.reshape(-1, width).astype(jnp.float32)
    grad_sum, grad_gain_second, grad_shift_second = norm_second_back(grad_out)
    grad_down_low = grad_sum.astype(jnp.bfloat16)
    grad_bias_down = jnp.sum(grad_down_low, axis=0, dtype=jnp.float32)
    grad_w_down = lax.dot_general(
        grad_down_low, activated_low, contract_rows, preferred_element_type=jnp.float32
    )
    grad_act = jnp.dot(grad_down_low, w_down, preferred_element_type=jnp.float32)
    grad_up = gate_back(grad_act)[0]
    grad_up_low = grad_up.astype(jnp.bfloat16)
    grad_bias_up = jnp.sum(grad_up_low, axis=0, dtype=jnp.float32)
    grad_w_up = lax.dot_general(
        normed_low, grad_up_low, contract_rows, preferred_element_type=jnp.float32
    )
    grad_normed = grad_sum + lax.dot_general(
        grad_up_low, w_up, contract_cols, preferred_element_type=jnp.float32
    )
    grad_first, grad_gain_first, grad_shift_first = norm_first_back(grad_normed)
    grad_attn_low = grad_first.astype(jnp.bfloat16)
    grad_bias_output = jnp.sum(grad_attn_low, axis=0, dtype=jnp.float32)
    grad_w_output = lax.dot_general(
        mixed_flat, grad_attn_low, contract_rows, preferred_element_type=jnp.float32
    )
    grad_mixed = lax.dot_general(
        grad_attn_low, w_output, contract_cols, preferred_element_type=jnp.float32
    )
    grad_heads = lax.all_to_all(
        shaped(grad_mixed.astype(jnp.bfloat16)), "seq", split_axis=2, concat_axis=1, tiled=True
    )

    def attend_back_one(packed):
        query_rows, key_rows, value_rows, grad_rows, mass_rows, length = packed
        return attend_back_span(
            query_rows, key_rows, value_rows, grad_rows, mass_rows, length, full_len
        )

    grad_q_heads, grad_k_heads, grad_v_heads = lax.map(
        attend_back_one,
        (
            heads_query.reshape(split_shape),
            heads_key.reshape(split_shape),
            heads_value.reshape(split_shape),
            grad_heads.reshape(split_shape),
            log_mass,
            counts,
        ),
    )
    heads_shape = (seqs_local, full_len, head_width)
    grad_q_tok, grad_k_tok, grad_v_tok = (
        lax.all_to_all(
            grad_q_heads.reshape(heads_shape), "seq", split_axis=1, concat_axis=2, tiled=True
        ),
        lax.all_to_all(
            grad_k_heads.reshape(heads_shape), "seq", split_axis=1, concat_axis=2, tiled=True
        ),
        lax.all_to_all(
            grad_v_heads.reshape(heads_shape), "seq", split_axis=1, concat_axis=2, tiled=True
        ),
    )
    grad_q_flat = grad_q_tok.reshape(-1, width)
    grad_k_flat = grad_k_tok.reshape(-1, width)
    grad_v_flat = grad_v_tok.reshape(-1, width)
    grad_w_query = lax.dot_general(
        tokens, grad_q_flat, contract_rows, preferred_element_type=jnp.float32
    )
    grad_w_key = lax.dot_general(
        tokens, grad_k_flat, contract_rows, preferred_element_type=jnp.float32
    )
    grad_w_value = lax.dot_general(
        tokens, grad_v_flat, contract_rows, preferred_element_type=jnp.float32
    )
    grad_bias_query = jnp.sum(grad_q_flat, axis=0, dtype=jnp.float32)
    grad_bias_value = jnp.sum(grad_v_flat, axis=0, dtype=jnp.float32)
    grad_tokens = grad_sum + grad_first
    grad_tokens = grad_tokens + lax.dot_general(
        grad_q_flat, w_query, contract_cols, preferred_element_type=jnp.float32
    )
    grad_tokens = grad_tokens + lax.dot_general(
        grad_k_flat, w_key, contract_cols, preferred_element_type=jnp.float32
    )
    grad_tokens = grad_tokens + lax.dot_general(
        grad_v_flat, w_value, contract_cols, preferred_element_type=jnp.float32
    )
    input_grad = grad_tokens.astype(jnp.bfloat16).reshape(inputs.shape)
    grad_att = jnp.stack([grad_w_query, grad_w_key, grad_w_value, grad_w_output]).reshape(
        4, width, batch_count, column_width
    )
    grad_feed = jnp.stack([grad_w_up, grad_w_down]).reshape(
        2, width, batch_count, seq_count, feed_width
    )
    grad_vec = jnp.concatenate(
        [
            jnp.stack([grad_bias_query, grad_bias_value, grad_bias_output]),
            grad_bias_up.reshape(4, width),
            jnp.stack(
                [
                    grad_bias_down,
                    grad_gain_first,
                    grad_shift_first,
                    grad_gain_second,
                    grad_shift_second,
                ]
            ),
        ],
        axis=0,
    ).reshape(12, batch_count, column_width)
    grad_att, grad_feed, grad_vec = (
        lax.psum_scatter(grad_att, "batch", scatter_dimension=2, tiled=True),
        lax.psum_scatter(grad_feed, "batch", scatter_dimension=2, tiled=True),
        lax.psum_scatter(grad_vec, "batch", scatter_dimension=1, tiled=True),
    )
    grad_att, grad_feed, grad_vec = (
        lax.psum_scatter(
            grad_att.astype(jnp.bfloat16), "seq", scatter_dimension=0, tiled=True
        ).astype(jnp.float32),
        lax.psum_scatter(
            grad_feed.astype(jnp.bfloat16), "seq", scatter_dimension=3, tiled=True
        ).astype(jnp.float32),
        lax.psum_scatter(
            grad_vec.astype(jnp.bfloat16), "seq", scatter_dimension=0, tiled=True
        ).astype(jnp.float32),
    )
    grad_att = grad_att.reshape(attention_local, width, column_width)
    grad_feed = grad_feed.reshape(2, width, feed_width)
    grad_vec = grad_vec.reshape(vector_rows, column_width)
    attention_moment = muon_decay * attention_momenta + grad_att
    feed_moment = muon_decay * feed_momenta + grad_feed
    gram_att, gram_feed = gram_sums(attention_moment, feed_moment)
    ortho_att, square_att = start_iterate(attention_moment, gram_att)
    ortho_feed, square_feed = start_iterate(feed_moment, gram_feed)
    for iteration in range(NS_STEPS):
        ortho_att = newton_turn(ortho_att, square_att)
        ortho_feed = newton_turn(ortho_feed, square_feed)
        if iteration + 1 < NS_STEPS:
            square_att, square_feed = gram_sums(ortho_att, ortho_feed)
    attention_next = attention_weights * (1.0 - muon_rate * decay_rate) - muon_rate * ortho_att
    feed_next = feed_weights * (1.0 - muon_rate * decay_rate) - muon_rate * ortho_feed
    vector_first_next = beta_one * vector_first + (1.0 - beta_one) * grad_vec
    vector_second_next = beta_two * vector_second + (1.0 - beta_two) * grad_vec * grad_vec
    first_hat = vector_first_next / (1.0 - beta_one**STEP)
    second_hat = vector_second_next / (1.0 - beta_two**STEP)
    vector_next = vector_params * (1.0 - adam_rate * decay_rate) - adam_rate * first_hat / (
        jnp.sqrt(second_hat) + adam_eps
    )
    return (
        layer_out,
        input_grad,
        attention_next,
        attention_moment,
        feed_next,
        feed_moment,
        vector_next,
        vector_first_next,
        vector_second_next,
    )


def solution(mesh):
    return jax.shard_map(
        shards,
        mesh=mesh,
        in_specs=(
            P("batch", "seq", None),
            P("batch"),
            P("batch", "seq", None),
            P("seq", None, "batch"),
            P("seq", None, "batch"),
            P(None, None, ("batch", "seq")),
            P(None, None, ("batch", "seq")),
            P("seq", "batch"),
            P("seq", "batch"),
            P("seq", "batch"),
        ),
        out_specs=(
            P("batch", "seq", None),
            P("batch", "seq", None),
            P("seq", None, "batch"),
            P("seq", None, "batch"),
            P(None, None, ("batch", "seq")),
            P(None, None, ("batch", "seq")),
            P("seq", "batch"),
            P("seq", "batch"),
            P("seq", "batch"),
        ),
        check_vma=False,
    )
```

profile of v0, /device:TPU:0, one launch (start us, length us, event | category | flops | bytes accessed | tf_op | source)
XLA Modules:
  0.0 1703.6 jit_solution(6892249541371819682)
XLA Ops:
  8.1 7.6 all-gather
  16.5 5.1 all-gather.5
  21.6 30.9 %all-gather.6 = bf16[8,64,12]{1,2,0:T(8,128)(2,1)S(1)} all-gather(bf16[1,64,12]{1,2,0:T(8,128)(2,1)S(1)} %bitcast.452), channel_id=5, replica_groups=mesh['batch'=8,'seq'=4] {'batch'}, dimensions={0}, use_global_device_ids=true | all-gather | bytes 13824 | tf_op jit(solution)/shard_map/all_gather | solution.py:142
  52.6 14.1 all-gather.12.cloned.1.call-done
  76.6 11.4 all-to-all-done.1
  94.8 11.1 all-to-all-done
  105.9 4.3 all-to-all-start.2
  110.2 18.5 %all-gather.4 = bf16[2,512,256]{1,2,0:T(8,128)(2,1)} all-gather(bf16[2,512,64]{1,2,0:T(8,128)(2,1)S(1)} %convert_element_type.129), channel_id=6, replica_groups=mesh['batch'=8,'seq'=4] {'seq'}, dimensions={2}, use_global_device_ids=true | all-gather | bytes 655360 | tf_op jit(solution)/shard_map/all_gather | solution.py:136
  136.3 22.3 %while.26 = (s32[]{:T(128)}, bf16[3,1024,2,64]{1,3,2,0:T(8,128)(2,1)S(1)}, f32[3,2,1024]{2,1,0:T(2,128)S(1)}, bf16[3,1024,2,64]{1,3,2,0:T(8,128)(2,1)S(1)}, s32[...) while((s32[]{:T(128)}, ...), condition=%wide.region_3.4_spmd, body=%wide.region_0.3_spmd.sunk | while | flops 562166784 | bytes 26286192 | solution.py:188
  160.0 4.2 all-to-all-start.3
  164.6 14.2 all-to-all-done.3
  183.5 16.5 all-gather.10.cloned.1.call-done
  211.0 6.1 convert_reduce_fusion
  226.0 4.3 pad_maximum_fusion
  237.8 18.1 %all_to_all.120 = bf16[3,256,512]{1,0,2:T(4,128)(2,1)S(1)} all-to-all(bf16[3,256,512]{1,0,2:T(4,128)(2,1)} %copy.134), channel_id=1, replica_groups=mesh['batch'=8,'seq'=4] {'seq'}, dimensions={2} | all-to-all | bytes 1572864 | tf_op jit(solution)/shard_map/all_to_all | solution.py:245
  262.9 49.1 %while.27 = (s32[]{:T(128)}, bf16[3,1024,2,64]{1,3,2,0:T(8,128)(2,1)}, bf16[3,1024,2,64]{1,3,2,0:T(8,128)(2,1)}, bf16[3,1024,2,64]{1,3,2,0:T(8,128)(2,1)}, bf16[...) while((s32[]{:T(128)}, ...), condition=%wide.region_14.15_spmd, body=%wide.region_12.14_spmd.sunk | while | flops 1374288896 | bytes 75039968 | solution.py:255
  320.4 11.9 all-to-all-done.5
  359.6 10.7 all-to-all-done.6
  377.3 168.6 %all-reduce.35 = (bf16[4,512,8,64]{1,3,2,0:T(8,128)(2,1)}, bf16[12,8,64]{2,1,0:T(8,128)(2,1)}) all-reduce(f32[4,512,8,64]{1,3,2,0:T(8,128)} %pad_maximum_fusion.1, f32[12,8,64]{2,1,0:T(8,128)S(1)} %constant_dynamic-update-slice_fusion), channel_id=7, replica_groups=mesh['batch'=8,'seq'=4] {'batch'}, use_global_device_ids=true, to_apply=%region_15.16.clone | all-reduce | flops 1054720 | bytes 6328320
  550.5 16.7 reduce-scatter.8.cloned.1.call-done
  570.2 21.1 %reduce-scatter.12.cloned.1.call-done = bf16[2,512,1,1,64]{1,4,0,3,2:T(8,128)(2,1)} async-done(((bf16[2,512,1,4,64]{1,4,0,3,2:T(8,128)(2,1)}), bf16[2,512,1,1,64]{1,4,0,3,2:T(8,128)(2,1)}) %reduce-scatter.12.cloned.1.call-update) | async-done | bytes 131088 | tf_op jit(solution)/shard_map/reduce_scatter | solution.py:334
  595.9 77.1 %all-reduce.16.cloned.1.call-done = f32[1,512,512]{2,1,0:T(8,128)} async-done(((f32[1,512,512]{2,1,0:T(8,128)}), f32[1,512,512]{2,1,0:T(8,128)}) %all-reduce.16.cloned.1.call-update) | async-done | bytes 1048592 | tf_op jit(solution)/shard_map/psum | solution.py:89
  681.4 130.4 %all-reduce.26.cloned.1.call-done = f32[2,512,512]{2,1,0:T(8,128)} async-done(((f32[2,512,512]{2,1,0:T(8,128)}), f32[2,512,512]{2,1,0:T(8,128)}) %all-reduce.26.cloned.1.call-update) | async-done | bytes 2097168 | tf_op jit(solution)/shard_map/psum | solution.py:90
  821.8 71.0 %all-reduce.18.cloned.1.call-done = f32[512,512]{1,0:T(8,128)} async-done(((f32[512,512]{1,0:T(8,128)}), f32[512,512]{1,0:T(8,128)}) %all-reduce.18.cloned.1.call-update) | async-done | bytes 1048592 | tf_op jit(solution)/shard_map/psum | solution.py:89
  899.8 131.8 %all-reduce.28.cloned.1.call-done = f32[2,512,512]{2,1,0:T(8,128)} async-done(((f32[2,512,512]{2,1,0:T(8,128)}), f32[2,512,512]{2,1,0:T(8,128)}) %all-reduce.28.cloned.1.call-update) | async-done | bytes 2097168 | tf_op jit(solution)/shard_map/psum | solution.py:90
  1042.1 70.2 %all-reduce.20.cloned.1.call-done = f32[512,512]{1,0:T(8,128)} async-done(((f32[512,512]{1,0:T(8,128)}), f32[512,512]{1,0:T(8,128)}) %all-reduce.20.cloned.1.call-update) | async-done | bytes 1048592 | tf_op jit(solution)/shard_map/psum | solution.py:89
  1122.2 128.9 %all-reduce.30.cloned.1.call-done = f32[2,512,512]{2,1,0:T(8,128)} async-done(((f32[2,512,512]{2,1,0:T(8,128)}), f32[2,512,512]{2,1,0:T(8,128)}) %all-reduce.30.cloned.1.call-update) | async-done | bytes 2097168 | tf_op jit(solution)/shard_map/psum | solution.py:90
  1263.2 68.8 %all-reduce.22.cloned.1.call-done = f32[512,512]{1,0:T(8,128)} async-done(((f32[512,512]{1,0:T(8,128)}), f32[512,512]{1,0:T(8,128)}) %all-reduce.22.cloned.1.call-update) | async-done | bytes 1048592 | tf_op jit(solution)/shard_map/psum | solution.py:89
  1340.2 6.6 all-reduce.2
  1346.8 123.9 %all-reduce.32.cloned.1.call-done = f32[2,512,512]{2,1,0:T(8,128)} async-done(((f32[2,512,512]{2,1,0:T(8,128)}), f32[2,512,512]{2,1,0:T(8,128)}) %all-reduce.32.cloned.1.call-update) | async-done | bytes 2097168 | tf_op jit(solution)/shard_map/psum | solution.py:90
  1485.1 66.3 %all-reduce.24.cloned.1.call-done = f32[512,512]{1,0:T(8,128)} async-done(((f32[512,512]{1,0:T(8,128)}), f32[512,512]{1,0:T(8,128)}) %all-reduce.24.cloned.1.call-update) | async-done | bytes 1048592 | tf_op jit(solution)/shard_map/psum | solution.py:89
  1556.8 133.2 %all-reduce.34.cloned.1.call-done = f32[2,512,512]{2,1,0:T(8,128)} async-done(((f32[2,512,512]{2,1,0:T(8,128)}), f32[2,512,512]{2,1,0:T(8,128)}) %all-reduce.34.cloned.1.call-update) | async-done | bytes 2097168 | tf_op jit(solution)/shard_map/psum | solution.py:90
  (313 shorter events, 283.2 us)
Async XLA Ops:
  7.2 59.5 %all-gather.12.cloned.1.call-start = ((), (), s32[]{:S(2)}) async-start(), calls=%async_computation.25 | async-start | bytes 2359296 | tf_op jit(solution)/shard_map/all_gather | solution.py:140
  70.0 18.0 %all-to-all-start.1 = ((bf16[3,256,512]{1,0,2:T(4,128)(2,1)}), bf16[3,256,512]{1,0,2:T(4,128)(2,1)S(1)}, u32[]{:S(2)}, u32[]{:S(2)}) async-start(bf16[3,256,512]{1,0,2:T(4,128)(2,1)} %copy.127), calls=%async_computation.1 | async-start | bytes 2097152 | tf_op jit(solution)/shard_map/all_to_all | solution.py:175
  87.9 18.0 %all-to-all-start = ((bf16[3,256,512]{1,0,2:T(4,128)(2,1)}), bf16[3,256,512]{1,0,2:T(4,128)(2,1)S(1)}, u32[]{:S(2)}, u32[]{:S(2)}) async-start(bf16[3,256,512]{1,0,2:T(4,128)(2,1)} %copy.125), calls=%async_computation | async-start | bytes 2097152 | tf_op jit(solution)/shard_map/all_to_all | solution.py:177
  93.3 16.9 copy-start.28
  105.9 27.6 %all-to-all-start.2 = ((bf16[3,256,512]{1,0,2:T(4,128)(2,1)}), bf16[3,256,512]{1,0,2:T(4,128)(2,1)}, u32[]{:S(2)}, u32[]{:S(2)}) async-start(bf16[3,256,512]{1,0,2:T(4,128)(2,1)} %copy.129), calls=%async_computation.2 | async-start | bytes 2097152 | tf_op jit(solution)/shard_map/all_to_all | solution.py:176
  110.1 89.8 %all-gather.10.cloned.1.call-start = ((), (), s32[]{:S(2)}) async-start(), calls=%async_computation.11 | async-start | bytes 4718592 | tf_op jit(solution)/shard_map/all_gather | solution.py:141
  158.6 21.6 %copy-start.12 = (bf16[3,1024,2,64]{1,3,2,0:T(8,128)(2,1)}, bf16[3,1024,2,64]{1,3,2,0:T(8,128)(2,1)S(1)}, u32[]{:S(2)}) copy-start(bf16[3,1024,2,64]{1,3,2,0:T(8,128)(2,1)S(1)} %get-tuple-element.386) | copy-start | bytes 2359300
  160.0 18.8 %all-to-all-start.3 = ((bf16[3,1024,128]{2,0,1:T(4,128)(2,1)}), bf16[3,1024,128]{2,0,1:T(4,128)(2,1)}, u32[]{:S(2)}, u32[]{:S(2)}) async-start(bf16[3,1024,128]{2,0,1:T(4,128)(2,1)} %copy.131), calls=%async_computation.3 | async-start | bytes 2097152 | tf_op jit(solution)/shard_map/all_to_all | solution.py:197
  164.3 384.0 %reduce-scatter.10.cloned.1.call-start = ((), (), s32[]{:S(2)}) async-start(), calls=%async_computation.18 | async-start | bytes 9437184 | tf_op jit(solution)/shard_map/reduce_scatter | solution.py:327
  183.1 21.3 %copy-start.10 = (f32[768,512]{1,0:T(8,128)}, f32[768,512]{1,0:T(8,128)S(1)}, u32[]{:S(2)}) copy-start(f32[768,512]{1,0:T(8,128)S(1)} %get-tuple-element.176) | copy-start | bytes 4718596
  314.4 18.0 %all-to-all-start.5 = ((bf16[3,1024,128]{2,0,1:T(4,128)(2,1)}), bf16[3,1024,128]{2,0,1:T(4,128)(2,1)S(1)}, u32[]{:S(2)}, u32[]{:S(2)}) async-start(bf16[3,1024,128]{2,0,1:T(4,128)(2,1)} %copy.136), calls=%async_computation.5 | async-start | bytes 2097152 | tf_op jit(solution)/shard_map/all_to_all | solution.py:268
  317.9 19.1 %copy-start.8 = (bf16[3,256,512]{2,1,0:T(8,128)(2,1)S(1)}, bf16[3,256,512]{2,1,0:T(8,128)(2,1)}, u32[]{:S(2)}) copy-start(bf16[3,256,512]{2,1,0:T(8,128)(2,1)} %param.16) | copy-start | bytes 2359300
  318.0 19.4 %copy-start.39 = (u32[32]{0:T(128)S(1)}, u32[32]{0:T(128)}, u32[]{:S(2)}) copy-start(u32[32]{0:T(128)} %constant.138) | copy-start | bytes 388
  333.3 18.1 %all-to-all-start.7 = ((bf16[3,1024,128]{2,0,1:T(4,128)(2,1)}), bf16[3,1024,128]{2,0,1:T(4,128)(2,1)S(1)}, u32[]{:S(2)}, u32[]{:S(2)}) async-start(bf16[3,1024,128]{2,0,1:T(4,128)(2,1)} %copy.142), calls=%async_computation.7 | async-start | bytes 2097152 | tf_op jit(solution)/shard_map/all_to_all | solution.py:274
  351.5 18.8 %all-to-all-start.6 = ((bf16[3,1024,128]{2,0,1:T(4,128)(2,1)}), bf16[3,1024,128]{2,0,1:T(4,128)(2,1)}, u32[]{:S(2)}, u32[]{:S(2)}) async-start(bf16[3,1024,128]{2,0,1:T(4,128)(2,1)} %copy.139), calls=%async_computation.6 | async-start | bytes 2097152 | tf_op jit(solution)/shard_map/all_to_all | solution.py:271
  355.8 211.5 %reduce-scatter.8.cloned.1.call-start = ((), (), s32[]{:S(2)}) async-start(), calls=%async_computation.12 | async-start | bytes 327680 | tf_op jit(solution)/shard_map/reduce_scatter | solution.py:331
  545.9 21.3 %copy-start.32 = (f32[1,512,64]{1,2,0:T(8,128)S(1)}, f32[1,512,64]{1,2,0:T(8,128)}, u32[]{:S(2)}) copy-start(f32[1,512,64]{1,2,0:T(8,128)} %param.18) | copy-start | bytes 393220
  548.2 43.0 %copy-start.31 = (f32[2,512,64]{1,2,0:T(8,128)S(1)}, f32[2,512,64]{1,2,0:T(8,128)}, u32[]{:S(2)}) copy-start(f32[2,512,64]{1,2,0:T(8,128)} %param.20) | copy-start | bytes 786436
  548.3 43.0 %reduce-scatter.12.cloned.1.call-start = ((), (), s32[]{:S(2)}) async-start(), calls=%async_computation.19 | async-start | bytes 655360 | tf_op jit(solution)/shard_map/reduce_scatter | solution.py:334
  550.4 122.6 %all-reduce.16.cloned.1.call-start = ((), (), s32[]{:S(2)}) async-start(), calls=%async_computation.13 | async-start | bytes 2097152 | tf_op jit(solution)/shard_map/psum | solution.py:89
  568.1 110.1 %copy-start.27 = (f32[1,512,64]{1,2,0:T(8,128)}, f32[1,512,64]{1,2,0:T(8,128)S(1)}, u32[]{:S(2)}) copy-start(f32[1,512,64]{1,2,0:T(8,128)S(1)} %convert_add_fusion.3) | copy-start | bytes 393220
  570.1 241.7 %all-reduce.26.cloned.1.call-start = ((), (), s32[]{:S(2)}) async-start(), calls=%async_computation.20 | async-start | bytes 4194304 | tf_op jit(solution)/shard_map/psum | solution.py:90
  592.2 224.1 %copy-start.9 = (f32[2,512,64]{1,2,0:T(8,128)}, f32[2,512,64]{1,2,0:T(8,128)S(1)}, u32[]{:S(2)}) copy-start(f32[2,512,64]{1,2,0:T(8,128)S(1)} %convert_add_fusion.2) | copy-start | bytes 786436
  595.4 297.4 %all-reduce.18.cloned.1.call-start = ((), (), s32[]{:S(2)}) async-start(), calls=%async_computation.14 | async-start | bytes 2097152 | tf_op jit(solution)/shard_map/psum | solution.py:89
  681.4 350.2 %all-reduce.28.cloned.1.call-start = ((), (), s32[]{:S(2)}) async-start(), calls=%async_computation.21 | async-start | bytes 4194304 | tf_op jit(solution)/shard_map/psum | solution.py:90
  821.8 290.6 %all-reduce.20.cloned.1.call-start = ((), (), s32[]{:S(2)}) async-start(), calls=%async_computation.15 | async-start | bytes 2097152 | tf_op jit(solution)/shard_map/psum | solution.py:89
  899.6 351.5 %all-reduce.30.cloned.1.call-start = ((), (), s32[]{:S(2)}) async-start(), calls=%async_computation.22 | async-start | bytes 4194304 | tf_op jit(solution)/shard_map/psum | solution.py:90
  1040.8 291.1 %all-reduce.22.cloned.1.call-start = ((), (), s32[]{:S(2)}) async-start(), calls=%async_computation.16 | async-start | bytes 2097152 | tf_op jit(solution)/shard_map/psum | solution.py:89
  1119.1 351.6 %all-reduce.32.cloned.1.call-start = ((), (), s32[]{:S(2)}) async-start(), calls=%async_computation.23 | async-start | bytes 4194304 | tf_op jit(solution)/shard_map/psum | solution.py:90
  1260.3 291.1 %all-reduce.24.cloned.1.call-start = ((), (), s32[]{:S(2)}) async-start(), calls=%async_computation.17 | async-start | bytes 2097152 | tf_op jit(solution)/shard_map/psum | solution.py:89
  1338.7 351.3 %all-reduce.34.cloned.1.call-start = ((), (), s32[]{:S(2)}) async-start(), calls=%async_computation.24 | async-start | bytes 4194304 | tf_op jit(solution)/shard_map/psum | solution.py:90
  1553.7 140.1 %copy-start.29 = (f32[2,512,64]{1,2,0:T(8,128)S(1)}, f32[2,512,64]{1,2,0:T(8,128)}, u32[]{:S(2)}) copy-start(f32[2,512,64]{1,2,0:T(8,128)} %param.19) | copy-start | bytes 786436
  (36 other events, 113.4 us)
Sparse Core Ops, SparseCore 0:
  15.9 50.7 all-gather.11
  128.8 71.1 all-gather.9
  230.4 147.1 reduce-scatter.9
  548.4 18.7 reduce-scatter.7
  569.5 21.6 reduce-scatter.11
  595.0 77.9 all-reduce.15
  678.4 133.3 all-reduce.25
  815.7 77.0 all-reduce.17
  898.2 133.4 all-reduce.27
  1035.4 76.8 all-reduce.19
  1117.7 133.3 all-reduce.29
  1254.9 77.0 all-reduce.21
  1337.3 133.3 all-reduce.31
  1474.5 76.8 all-reduce.23
  1556.6 133.3 all-reduce.33
where the time goes:
time: 1710 us; the launch traced here: 1700 us
  waiting for transfers between devices  1130 us (66%)
  blocking collectives  255 us (15%)
  matrix products  166 us (10%)
  local copies, waits for them, and re-layouts  59 us (3%)
  other arithmetic  45.1 us (3%)
  starting transfers between devices  28.7 us (2%)
    psum x5, waiting for transfers between devices, gram_sums(): gram_feed = lax.psum(gram_of(part_feed), ('batch', 'seq'))  648 us
    psum x5, waiting for transfers between devices, gram_sums(): gram_att = lax.psum(gram_of(part_att), 'batch')  353 us
    unnamed x2, blocking collectives  175 us
  transfers between devices with their start and end apart: 22, of which 20 were waited for; matrix products, arithmetic and copies ran while one was open for 13% of the time, Pallas kernels for 0%

commit v1 on v0

v1 whole, which is shorter than its diff:
```python
import functools

import jax
import jax.numpy as jnp
from jax import lax
from jax.experimental import pallas as pl
from jax.experimental.pallas import tpu as pltpu
from jax.sharding import PartitionSpec as P

HEAD_DIM = 64
STEP = 10
NS_STEPS = 5

newton_coef = (3.4445, -4.775, 2.0315)
muon_rate = 0.6
muon_decay = 0.95
adam_rate = 0.3
beta_one = 0.9
beta_two = 0.999
decay_rate = 0.01
adam_eps = 1e-08
norm_eps = 1e-05
masked_score = -1e30
bf16 = jnp.bfloat16
f32 = jnp.float32
VMEM_LIMIT = 60 * 1024 * 1024

NN = (((1,), (0,)), ((), ()))
NT = (((1,), (1,)), ((), ()))
TN = (((0,), (0,)), ((), ()))


def dot(left, right, dims=NN):
    return lax.dot_general(left, right, dims, preferred_element_type=f32)


def xor_permute(value, axis, step):
    count = lax.axis_size(axis)
    return lax.ppermute(value, axis, [(i, i ^ step) for i in range(count)])


def halves(value):
    high = value.astype(bf16)
    return high, (value - high.astype(f32)).astype(bf16)


def dot_split(left, right, dims=NN):
    (left_high, left_low), (right_high, right_low) = left, right
    return (
        dot(left_high, right_high, dims)
        + dot(left_high, right_low, dims)
        + dot(left_low, right_high, dims)
    )


def newton_loop(square, rows):
    for turn in range(NS_STEPS):
        square_parts = halves(square)
        poly = newton_coef[1] * square + newton_coef[2] * dot_split(square_parts, square_parts)
        poly_parts = halves(poly)
        rows = newton_coef[0] * rows + dot_split(halves(rows), poly_parts)
        if turn + 1 < NS_STEPS:
            once = newton_coef[0] * square + dot_split(poly_parts, square_parts)
            square = newton_coef[0] * once + dot_split(halves(once), poly_parts)
    return rows


def newton_kernel(square_ref, rows_ref, out_ref):
    gram = square_ref[...]
    width = gram.shape[0]
    on_diagonal = lax.broadcasted_iota(jnp.int32, (width, width), 0) == lax.broadcasted_iota(
        jnp.int32, (width, width), 1
    )
    trace = jnp.sum(jnp.where(on_diagonal, gram, 0.0), keepdims=True)
    factor = 1.0 / (jnp.sqrt(trace) + 1e-07)
    out_ref[...] = newton_loop(gram * (factor * factor), rows_ref[...] * factor)


def gram_of_rows(rows):
    parts = halves(rows)
    return dot_split(parts, parts, TN)


def gram_kernel(rows_ref, out_ref):
    out_ref[...] = gram_of_rows(rows_ref[...])


def gram(rows):
    width = rows.shape[1]
    return pl.pallas_call(
        gram_kernel,
        out_shape=jax.ShapeDtypeStruct((width, width), f32),
        in_specs=[pl.BlockSpec(memory_space=pltpu.VMEM)],
        out_specs=pl.BlockSpec(memory_space=pltpu.VMEM),
        compiler_params=pltpu.CompilerParams(vmem_limit_bytes=VMEM_LIMIT),
        name="gram",
    )(rows)


def newton(gram, rows):
    return pl.pallas_call(
        newton_kernel,
        out_shape=jax.ShapeDtypeStruct(rows.shape, f32),
        in_specs=[pl.BlockSpec(memory_space=pltpu.VMEM)] * 2,
        out_specs=pl.BlockSpec(memory_space=pltpu.VMEM),
        compiler_params=pltpu.CompilerParams(vmem_limit_bytes=VMEM_LIMIT),
        name="newton",
    )(gram, rows)


def layer_norm(values_in, gain_vec, shift_vec):
    centre = values_in - jnp.mean(values_in, axis=-1, keepdims=True)
    inverse_dev = lax.rsqrt(jnp.mean(centre * centre, axis=-1, keepdims=True) + norm_eps)
    return centre * inverse_dev * gain_vec + shift_vec


def smooth_gate(values_in):
    return jax.nn.gelu(values_in, approximate=True)


def masked_scores(query_rows, key_rows, length):
    raw_scores = jnp.einsum("qhd,khd->hqk", query_rows, key_rows, preferred_element_type=f32)
    raw_scores = raw_scores * query_rows.shape[2] ** (-0.5)
    live_keys = jnp.arange(key_rows.shape[0]) < length
    return jnp.where(live_keys[None, None, :], raw_scores, masked_score)


def attend(query_rows, key_rows, value_rows, length):
    scores = masked_scores(query_rows, key_rows, length)
    highest_score = jnp.max(scores, axis=2, keepdims=True)
    exponents = jnp.exp(scores - highest_score)
    total_mass = jnp.sum(exponents, axis=2, keepdims=True)
    weights_low = (exponents / total_mass).astype(bf16)
    mixed = jnp.einsum("hqk,khd->qhd", weights_low, value_rows, preferred_element_type=f32)
    log_mass = (highest_score + jnp.log(total_mass))[:, :, 0]
    return (mixed.astype(bf16), log_mass)


def attend_back(query_rows, key_rows, value_rows, grad_mixed, log_mass, length):
    scores = masked_scores(query_rows, key_rows, length)
    weights = jnp.exp(scores - log_mass[:, :, None])
    grad_weights = jnp.einsum("qhd,khd->hqk", grad_mixed, value_rows, preferred_element_type=f32)
    inner_sum = jnp.sum(weights * grad_weights, axis=2, keepdims=True)
    grad_scores = (weights * (grad_weights - inner_sum)).astype(bf16)
    scale = query_rows.shape[2] ** (-0.5)
    grad_query = jnp.einsum("hqk,khd->qhd", grad_scores, key_rows, preferred_element_type=f32)
    grad_key = jnp.einsum("hqk,qhd->khd", grad_scores, query_rows, preferred_element_type=f32)
    grad_value = jnp.einsum(
        "hqk,qhd->khd", weights.astype(bf16), grad_mixed, preferred_element_type=f32
    )
    return (
        (grad_query * scale).astype(bf16),
        (grad_key * scale).astype(bf16),
        grad_value.astype(bf16),
    )


def weights_to_heads(payload, batch_index):
    batch_count, seq_count = lax.axis_size("batch"), lax.axis_size("seq")
    blocks = batch_count // seq_count
    pieces = []
    for turn in range(batch_count):
        route = []
        for block in range(batch_count):
            for member in range(seq_count):
                target = (member * blocks + block % blocks) ^ turn
                route.append(
                    (block * seq_count + member, target * seq_count + block // blocks)
                )
        pieces.append(lax.ppermute(payload, ("batch", "seq"), route))
    stacked = jnp.stack(pieces)
    return jnp.take(stacked, batch_index ^ jnp.arange(batch_count), axis=0)


def gather_relative(value, axis, order):
    pieces = [(0, value)]
    for step in order:
        pieces = pieces + [(offset ^ step, xor_permute(piece, axis, step)) for offset, piece in pieces]
    return pieces


def gather_direct(value, axis):
    count = lax.axis_size(axis)
    return [value] + [xor_permute(value, axis, step) for step in range(1, count)]


def natural(pieces, index):
    return jnp.take(jnp.stack(pieces), index ^ jnp.arange(len(pieces)), axis=0)


def sum_gram(part):
    low_count = 2
    width = part.shape[0]
    batch_count = lax.axis_size("batch")
    mine = lax.axis_index("seq") % low_count
    two = part.reshape(low_count, width // low_count, width)
    keep = lax.dynamic_index_in_dim(two, mine, 0, keepdims=False)
    send = lax.dynamic_index_in_dim(two, 1 - mine, 0, keepdims=False)
    half = keep + xor_permute(send, "seq", 1)
    rows = half.shape[0] // batch_count
    chunks = lax.all_to_all(
        half.reshape(batch_count, rows, width), "batch", split_axis=0, concat_axis=0, tiled=True
    )
    own = jnp.sum(chunks, axis=0)
    half = natural(gather_direct(own, "batch"), lax.axis_index("batch")).reshape(half.shape)
    other = xor_permute(half, "seq", 1)
    first = jnp.where(mine == 0, half, other)
    second = jnp.where(mine == 0, other, half)
    return jnp.concatenate([first, second], axis=0)


def shards(
    inputs,
    counts,
    cotangent,
    attention_weights,
    attention_momenta,
    feed_weights,
    feed_momenta,
    vector_params,
    vector_first,
    vector_second,
):
    seqs, local_len, width = inputs.shape
    seq_count, batch_count = lax.axis_size("seq"), lax.axis_size("batch")
    seq_index, batch_index = lax.axis_index("seq"), lax.axis_index("batch")
    full_len = local_len * seq_count
    tokens_count = seqs * local_len
    head_width = width // seq_count
    head_count = head_width // HEAD_DIM
    column_width = attention_weights.shape[2]
    feed_width = feed_weights.shape[2]
    hidden = feed_width * batch_count * seq_count
    vector_rows = vector_params.shape[0]

    att_own = attention_weights[0].T
    feed_own = feed_weights.transpose(0, 2, 1)
    moment_own = attention_momenta[0].T
    feed_moment_own = feed_momenta.transpose(0, 2, 1)
    vec_low = vector_params.astype(bf16)

    feed_all, vec_all = (
        lax.all_gather(feed_own.astype(bf16), ("seq", "batch"), axis=1, tiled=False),
        lax.all_gather(vec_low, ("seq", "batch"), axis=0, tiled=False),
    )
    moment_all = lax.all_gather(moment_own, "batch", axis=0, tiled=True)
    x_parts = gather_relative(inputs, "seq", [2, 1])
    x_parts = [piece for _, piece in sorted(x_parts, key=lambda pair: pair[0])]
    pad = jnp.zeros((16, width), bf16).at[0, : vector_rows * column_width].set(vec_low.reshape(-1))
    payload = jnp.concatenate([att_own.astype(bf16), pad], axis=0)
    head_parts = weights_to_heads(payload, batch_index)
    head_weights = head_parts[:, :column_width].reshape(seq_count, head_width, width)
    first_vecs = head_parts[: batch_count // seq_count, column_width, : vector_rows * column_width]
    first_vecs = first_vecs.reshape(-1, vector_rows, column_width).transpose(1, 0, 2)
    first_vecs = first_vecs.reshape(vector_rows, head_width).astype(f32)
    output_parts = gather_direct(head_weights[3], "seq")
    w_output_t = natural(output_parts, seq_index).reshape(width, width)
    vec_full = vec_all.reshape(seq_count, batch_count, vector_rows, column_width)
    vec_full = vec_full.transpose(0, 2, 1, 3).reshape(12, width).astype(f32)
    w_up_t = feed_all[0].reshape(hidden, width)
    w_down = feed_all[1].reshape(hidden, width)
    bias_up = vec_full[3:7].reshape(batch_count, seq_count, feed_width)
    bias_up = bias_up.transpose(1, 0, 2).reshape(hidden)
    bias_output, bias_down = vec_full[2], vec_full[7]
    gain_first, shift_first, gain_second, shift_second = (vec_full[row] for row in range(8, 12))

    upper = seq_count // 2
    matrix = seq_index // upper
    moment_send = lax.dynamic_index_in_dim(feed_moment_own, 1 - matrix, 0, keepdims=False)
    moment_keep = lax.dynamic_index_in_dim(feed_moment_own, matrix, 0, keepdims=False)
    moment_other = xor_permute(moment_send, "seq", upper)

    x_all = natural(x_parts, seq_index).transpose(1, 0, 2, 3).reshape(seqs, full_len, width)

    def project(part, bias):
        value = lax.dot_general(
            x_all, head_weights[part], (((2,), (1,)), ((), ())), preferred_element_type=f32
        )
        if bias is not None:
            value = value + bias
        return value.astype(bf16).reshape(seqs, full_len, head_count, HEAD_DIM)

    query = project(0, first_vecs[0])
    key = project(1, None)
    value = project(2, first_vecs[1])
    mixed_heads, log_mass = lax.map(lambda args: attend(*args), (query, key, value, counts))
    mixed_out = mixed_heads.reshape(seqs, seq_count, local_len, head_width).transpose(1, 0, 2, 3)
    mixed_tok = lax.all_to_all(mixed_out, "seq", split_axis=0, concat_axis=0, tiled=True)
    mixed_flat = mixed_tok.transpose(1, 2, 0, 3).reshape(tokens_count, width)

    tokens = inputs.reshape(tokens_count, width)
    attn_out = dot(mixed_flat, w_output_t, NT) + bias_output
    first_in = tokens.astype(f32) + attn_out
    normed, norm_first_back = jax.vjp(layer_norm, first_in, gain_first, shift_first)
    normed_low = normed.astype(bf16)
    up_pre = dot(normed_low, w_up_t, NT) + bias_up
    activated, gate_back = jax.vjp(smooth_gate, up_pre)
    activated_low = activated.astype(bf16)
    down_out = dot(activated_low, w_down) + bias_down
    summed = tokens.astype(f32) + normed + down_out
    result, norm_second_back = jax.vjp(layer_norm, summed, gain_second, shift_second)
    layer_out = result.astype(bf16).reshape(inputs.shape)
    grad_out = cotangent.reshape(tokens_count, width).astype(f32)
    grad_sum, grad_gain_second, grad_shift_second = norm_second_back(grad_out)
    grad_down_low = grad_sum.astype(bf16)
    grad_bias_down = jnp.sum(grad_down_low, axis=0, dtype=f32)
    grad_w_down = dot(activated_low, grad_down_low, TN).astype(bf16)
    grad_act = dot(grad_down_low, w_down, NT)
    grad_up_low = gate_back(grad_act)[0].astype(bf16)
    grad_bias_up = jnp.sum(grad_up_low, axis=0, dtype=f32)
    grad_w_up = dot(grad_up_low, normed_low, TN).astype(bf16)
    grad_normed = grad_sum + dot(grad_up_low, w_up_t)
    grad_first, grad_gain_first, grad_shift_first = norm_first_back(grad_normed)
    grad_attn_low = grad_first.astype(bf16)
    grad_bias_output = jnp.sum(grad_attn_low, axis=0, dtype=f32)
    grad_w_output = dot(grad_attn_low, mixed_flat, TN).astype(bf16)
    grad_mixed = dot(grad_attn_low, w_output_t).astype(bf16)
    grad_mixed = grad_mixed.reshape(seqs, local_len, seq_count, head_width).transpose(2, 0, 1, 3)
    grad_heads = lax.all_to_all(grad_mixed, "seq", split_axis=0, concat_axis=0, tiled=True)
    grad_heads = grad_heads.transpose(1, 0, 2, 3).reshape(seqs, full_len, head_count, HEAD_DIM)

    low_index = seq_index % upper
    feed_grads = jnp.stack([grad_w_up, grad_w_down])
    feed_grads = feed_grads.reshape(2, seq_count // upper, upper, -1, width)
    pair_keep = lax.dynamic_index_in_dim(feed_grads, low_index, 2, keepdims=False)
    pair_send = lax.dynamic_index_in_dim(feed_grads, low_index ^ 1, 2, keepdims=False)
    pair_sum = (pair_keep.astype(f32) + xor_permute(pair_send, "seq", 1).astype(f32)).astype(bf16)
    cross_keep = lax.dynamic_index_in_dim(pair_sum, matrix, 0, keepdims=False)
    cross_send = lax.dynamic_index_in_dim(pair_sum, 1 - matrix, 0, keepdims=False)
    cross_sum = cross_keep.astype(f32) + xor_permute(cross_send, "seq", upper).astype(f32)
    cross_sum = cross_sum.astype(bf16).reshape(2, batch_count, feed_width, width)
    feed_chunks = lax.all_to_all(
        cross_sum.transpose(1, 0, 2, 3), "batch", split_axis=0, concat_axis=0, tiled=True
    )
    feed_sum = jnp.sum(feed_chunks.astype(f32), axis=0)
    mine_first = matrix == 0
    moment_pair = jnp.where(
        mine_first, jnp.stack([moment_keep, moment_other]), jnp.stack([moment_other, moment_keep])
    )
    feed_moment_pair = muon_decay * moment_pair + feed_sum
    feed_rows = feed_moment_pair.reshape(2 * feed_width, width)
    gram_feed = sum_gram(gram(feed_rows))
    ortho_feed_pair = newton(gram_feed, feed_rows).reshape(2, feed_width, width)
    both_pair = jnp.stack([feed_moment_pair, ortho_feed_pair], axis=1)
    both_keep = lax.dynamic_index_in_dim(both_pair, matrix, 0, keepdims=False)
    both_send = lax.dynamic_index_in_dim(both_pair, 1 - matrix, 0, keepdims=False)
    both_other = xor_permute(both_send, "seq", upper)
    both = jnp.where(
        mine_first, jnp.stack([both_keep, both_other], 1), jnp.stack([both_other, both_keep], 1)
    )
    feed_moment = both[0].transpose(0, 2, 1)
    ortho_feed = both[1].transpose(0, 2, 1)

    grad_query, grad_key, grad_value = lax.map(
        lambda args: attend_back(*args), (query, key, value, grad_heads, log_mass, counts)
    )
    flat_x = x_all.reshape(-1, width)
    head_grads = [
        grad.reshape(-1, head_width) for grad in (grad_query, grad_key, grad_value)
    ]
    head_weight_grads = [dot(grad, flat_x, TN).astype(bf16) for grad in head_grads]
    back_part = sum(dot(grad, head_weights[i]) for i, grad in enumerate(head_grads))
    back_part = back_part.astype(bf16).reshape(seqs, seq_count, local_len, width)
    back_part = jnp.take(back_part, seq_index ^ jnp.arange(seq_count), axis=1)
    low_half = [back_part[:, 0].astype(f32), back_part[:, upper].astype(f32)]
    low_got = xor_permute(
        jnp.stack([back_part[:, 1], back_part[:, upper + 1]]), "seq", 1
    ).astype(f32)
    high_got = xor_permute((low_half[1] + low_got[1]).astype(bf16), "seq", upper).astype(f32)
    grad_tokens = (grad_sum + grad_first).reshape(inputs.shape)
    input_grad = (grad_tokens + low_half[0] + low_got[0] + high_got).astype(bf16)

    output_chunks = lax.all_to_all(
        grad_w_output.reshape(seq_count, head_width, width),
        "seq",
        split_axis=0,
        concat_axis=0,
        tiled=True,
    )
    output_sum = jnp.sum(output_chunks.astype(f32), axis=0).astype(bf16)
    att_grads = jnp.stack(head_weight_grads + [output_sum])
    att_grads = att_grads.reshape(seq_count, batch_count, -1, 128).transpose(1, 0, 2, 3)

    def at_heads(grad):
        return lax.dynamic_update_slice(
            jnp.zeros((width,), f32), jnp.sum(grad, axis=0, dtype=f32), (seq_index * head_width,)
        )

    vec_grads = jnp.concatenate(
        [
            jnp.stack([at_heads(head_grads[0]), at_heads(head_grads[2]), grad_bias_output]),
            grad_bias_up.reshape(seq_count, batch_count, feed_width)
            .transpose(1, 0, 2)
            .reshape(4, width),
            jnp.stack(
                [
                    grad_bias_down,
                    grad_gain_first,
                    grad_shift_first,
                    grad_gain_second,
                    grad_shift_second,
                ]
            ),
        ]
    )
    vec_grads = vec_grads.astype(bf16).reshape(seq_count, vector_rows, batch_count, column_width)
    vec_grads = vec_grads.transpose(2, 0, 1, 3).reshape(batch_count, seq_count, -1)
    vec_grads = jnp.pad(vec_grads, ((0, 0), (0, 0), (0, 2048 - vec_grads.shape[2])))
    vec_grads = vec_grads.reshape(batch_count, seq_count, 16, 128)
    att_rows = att_grads.shape[2]
    payload = jnp.concatenate([att_grads, vec_grads], axis=2)
    payload = payload.reshape(batch_count * seq_count, att_rows + 16, 128)
    got = lax.all_to_all(payload, ("batch", "seq"), split_axis=0, concat_axis=0, tiled=True)
    got = got.reshape(batch_count, seq_count, att_rows + 16, 128).astype(f32)
    att_sum = jnp.sum(got[:, :, :att_rows], axis=0).astype(bf16)
    grad_vec = jnp.sum(got[:, :, att_rows:], axis=(0, 1)).reshape(-1)
    grad_vec = grad_vec[: vector_rows * column_width].reshape(vector_rows, column_width)
    att_full = natural(gather_direct(att_sum, "batch"), batch_index)
    att_full = att_full.transpose(1, 0, 2, 3).reshape(width, width)
    att_rows_all = muon_decay * moment_all + att_full.astype(f32)
    gram_att = gram(att_rows_all)
    att_rows_own = lax.dynamic_slice_in_dim(att_rows_all, batch_index * column_width, column_width)
    ortho_att = newton(gram_att, att_rows_own).T[None]
    attention_moment = att_rows_own.T[None]

    attention_next = attention_weights * (1.0 - muon_rate * decay_rate) - muon_rate * ortho_att
    feed_next = feed_weights * (1.0 - muon_rate * decay_rate) - muon_rate * ortho_feed
    vector_first_next = beta_one * vector_first + (1.0 - beta_one) * grad_vec
    vector_second_next = beta_two * vector_second + (1.0 - beta_two) * grad_vec * grad_vec
    first_hat = vector_first_next / (1.0 - beta_one**STEP)
    second_hat = vector_second_next / (1.0 - beta_two**STEP)
    vector_next = vector_params * (1.0 - adam_rate * decay_rate) - adam_rate * first_hat / (
        jnp.sqrt(second_hat) + adam_eps
    )
    return (
        layer_out,
        input_grad,
        attention_next,
        attention_moment,
        feed_next,
        feed_moment,
        vector_next,
        vector_first_next,
        vector_second_next,
    )


def solution(mesh):
    tokens_spec = P("batch", "seq", None)
    attention_spec = P("seq", None, "batch")
    feed_spec = P(None, None, ("batch", "seq"))
    vector_spec = P("seq", "batch")
    return jax.shard_map(
        shards,
        mesh=mesh,
        in_specs=(tokens_spec, P("batch"), tokens_spec)
        + (attention_spec,) * 2
        + (feed_spec,) * 2
        + (vector_spec,) * 3,
        out_specs=(tokens_spec,) * 2
        + (attention_spec,) * 2
        + (feed_spec,) * 2
        + (vector_spec,) * 3,
        check_vma=False,
    )
```

time: 1710 us -> 530 us (0.31)
  waiting for transfers between devices: 1130 us -> 63.8 us
  blocking collectives: 255 us -> 65.8 us
  matrix products: 166 us -> 86.5 us
  starting transfers between devices: 28.7 us -> 91.4 us
  other arithmetic: 45.1 us -> 83.6 us
  Pallas kernels: 0 us -> 36.8 us
  local copies, waits for them, and re-layouts: 59 us -> 81.6 us
    psum x10 -> x0, waiting for transfers between devices: 1000 us -> none  [the longest x5 648 us: gram_sums(): gram_feed = lax.psum(gram_of(part_feed), ('batch', 'seq'))]
    unnamed x2 -> x0, blocking collectives: 175 us -> none
    dot_general x69 -> x39, matrix products: 166 us -> 86.5 us  [the longest x15 36.4 us: dot(): return lax.dot_general(left, right, dims, preferred_element_type=f32)]
    ppermute x0 -> x36, waiting for transfers between devices: none -> 52.1 us  [the longest x28 48.1 us: xor_permute(): return lax.ppermute(value, axis, [(i, i ^ step) for i in range(count)])]
    all_to_all x7 -> x6, waiting for transfers between devices: 62.9 us -> 11.7 us  [the longest x1 7.74 us: shards(): lax.all_to_all(mixed_out, 'seq', split_axis=0, concat_axis=0, tiled=True)]
    ppermute x0 -> x36, starting transfers between devices: none -> 50.3 us  [the longest x28 36.5 us: xor_permute(): return lax.ppermute(value, axis, [(i, i ^ step) for i in range(count)])]
    reduce_scatter x3 -> x0, waiting for transfers between devices: 37.8 us -> none  [the longest x1 21.1 us: shards(): lax.psum_scatter(grad_feed.astype(jnp.bfloat16), 'seq', scatter_dimension...]
    pallas_call x0 -> x4, Pallas kernels: none -> 36.8 us  [the longest x2 31 us: newton(): pl.pallas_call(newton_kernel, out_shape=jax.ShapeDtypeStruct(rows.shape,...]
  transfers between devices with their start and end apart: 22 -> 44, of which waited for: 20 -> 10; matrix products, arithmetic and copies ran while one was open for 13% -> 45% of each run, Pallas kernels for 0% -> 7%
where the time goes in v1:
time: 530 us; the launch traced here: 526 us
  starting transfers between devices  91.4 us (17%)
  matrix products  86.5 us (16%)
  other arithmetic  83.6 us (16%)
  local copies, waits for them, and re-layouts  81.6 us (15%)
  blocking collectives  65.8 us (12%)
  waiting for transfers between devices  63.8 us (12%)
  Pallas kernels  36.8 us (7%)
  between operations  15.8 us (3%)
    all_gather x1, blocking collectives, shards(): lax.all_gather(vec_low, ('seq', 'batch'), axis=0, tiled=False)  65.8 us
    ppermute x28, waiting for transfers between devices, xor_permute(): return lax.ppermute(value, axis, [(i, i ^ step) for i in range(count)])  48.1 us
    ppermute x28, starting transfers between devices, xor_permute(): return lax.ppermute(value, axis, [(i, i ^ step) for i in range(count)])  36.5 us
    dot_general x15, matrix products, dot(): return lax.dot_general(left, right, dims, preferred_element_type=f32)  36.4 us
    pallas_call x2, Pallas kernels, newton(): pl.pallas_call(newton_kernel, out_shape=jax.ShapeDtypeStruct(rows.shape,...  31 us
    unnamed x152, local copies, waits for them, and re-layouts  20.7 us
    all_to_all x1, starting transfers between devices, shards(): lax.all_to_all(mixed_out, 'seq', split_axis=0, concat_axis=0, tiled=True)  15.9 us
    ppermute x8, starting transfers between devices, weights_to_heads(): pieces.append(lax.ppermute(payload, ('batch', 'seq'), route))  13.7 us
  transfers between devices with their start and end apart: 44, of which 10 were waited for; matrix products, arithmetic and copies ran while one was open for 45% of the time, Pallas kernels for 7%

profile of v1, /device:TPU:0, one launch (start us, length us, event | category | flops | bytes accessed | tf_op | source)
XLA Modules:
  0.0 525.7 jit_solution(8111486236208496448)
XLA Ops:
  14.4 4.0 collective-permute-start.5
  18.4 5.8 %collective-permute-start.7 = (bf16[80,512]{1,0:T(8,128)(2,1)S(1)}, bf16[80,512]{1,0:T(8,128)(2,1)S(1)}, u32[]{:S(2)}, u32[]{:S(2)}) collective-permute-start(bf16[80,512]{1,0:T(8,128)(2,1)S(1)} %fusion.102), channel_id=1, source_target_pairs={{0,16},{1,24},{2,0},{3,8},{4,20},{5,28},{6,4},{7,12},{8,17},{9,25}... | collective-permute-start | bytes 245768 | tf_op jit(solution)/shard_map/ppermute | solution.py:170
  25.1 65.8 %all-gather.2 = bf16[32,3,64]{2,1,0:T(4,128)(2,1)S(1)} all-gather(bf16[1,3,64]{2,1,0:T(4,128)(2,1)S(1)} %convert_bitcast_fusion.3), channel_id=2, replica_groups=mesh['batch'=8,'seq'=4] {'seq','batch'}, dimensions={0}, use_global_device_ids=true | all-gather | bytes 12672 | tf_op jit(solution)/shard_map/all_gather | solution.py:244
  99.6 4.0 collective-permute-done.8
  103.5 3.3 collective-permute-start.23
  106.9 13.0 %collective-permute-done.1 = bf16[3,256,512]{2,1,0:T(8,128)(2,1)S(1)} collective-permute-done((bf16[3,256,512]{2,1,0:T(8,128)(2,1)S(1)}, bf16[3,256,512]{2,1,0:T(8,128)(2,1)S(1)}, u32[]{:S(2)}, u32[]{:S(2)}) %collective-permute-start.1) | collective-permute-done | bytes 786464 | tf_op jit(solution)/shard_map/ppermute | solution.py:39
  137.3 22.3 %while.27 = (s32[]{:T(128)}, bf16[3,1024,2,64]{1,3,2,0:T(8,128)(2,1)S(1)}, f32[3,2,1024]{2,1,0:T(2,128)S(1)}, bf16[3,1024,2,64]{1,3,2,0:T(8,128)(2,1)S(1)}, s32[...) while((s32[]{:T(128)}, ...), condition=%wide.region_3.4_spmd, body=%wide.region_0.3_spmd.sunk | while | flops 562166784 | bytes 26286184 | solution.py:286
  163.3 15.9 %all-to-all-start = ((bf16[4,3,256,128]{3,2,1,0:T(8,128)(2,1)}), bf16[4,3,256,128]{3,2,1,0:T(8,128)(2,1)}, u32[]{:S(2)}, u32[]{:S(2)}) async-start(bf16[4,3,256,128]{3,2,1,0:T(8,128)(2,1)} %copy.90), calls=%async_computation | async-start | bytes 1572864 | tf_op jit(solution)/shard_map/all_to_all | solution.py:288
  182.9 7.7 %all-to-all-done = bf16[4,3,256,128]{3,2,1,0:T(8,128)(2,1)} async-done(((bf16[4,3,256,128]{3,2,1,0:T(8,128)(2,1)}), bf16[4,3,256,128]{3,2,1,0:T(8,128)(2,1)}, u32[]{:S(2)}, u32[]{:S(2)}) %all-to-all-start) | async-done | bytes 786464 | tf_op jit(solution)/shard_map/all_to_all | solution.py:288
  195.7 3.6 fusion.75
  205.2 6.1 %fusion.120 = (bf16[2048]{0:T(1024)(128)(2,1)S(1)}, bf16[768,2048]{1,0:T(8,128)(2,1)S(1)}) fusion(f32[768,2048]{1,0:T(8,128)S(1)} %fusion.75, f32[2048]{0:T(1024)S(1)} %copy-done.41, bf16[768,512]{1,0:T(8,128)(2,1)S(1)} %get-tuple-element.163, bf16[2,2048,512]{2,1,0:T(8,128)(2,1)S(1)} %copy-done.59), kind=kOutput, calls=%fused_computation.266 | convolution fusion | flops 1645213696 | bytes 12333056 | tf_op jit(solution)/shard_map/dot_general | solution.py:34
  217.1 4.1 all-to-all-start.2
  221.2 7.5 %convolution_convert_fusion = bf16[2048,512]{1,0:T(8,128)(2,1)} fusion(bf16[768,512]{1,0:T(8,128)(2,1)} %copy-done.32, f32[768,2048]{1,0:T(8,128)} %copy-done.61, f32[2048]{0:T(1024)S(1)} %copy-done.41), kind=kOutput, calls=%fused_computation.90 | convolution fusion | flops 1627389952 | bytes 9183232 | tf_op jit(solution)/shard_map/dot_general | solution.py:34
  234.8 4.6 all-to-all-start.1
  239.4 4.4 convolution_convert_fusion.1
  257.6 48.5 %while.28 = (s32[]{:T(128)}, bf16[3,1024,2,64]{1,3,2,0:T(8,128)(2,1)}, bf16[3,1024,2,64]{1,3,2,0:T(8,128)(2,1)}, bf16[3,1024,2,64]{1,3,2,0:T(8,128)(2,1)}, bf16[...) while((s32[]{:T(128)}, ...), condition=%wide.region_14.15_spmd, body=%wide.region_12.14_spmd.sunk | while | flops 1374288896 | bytes 65602688 | solution.py:354
  260.1 3.5 multiply_reduce_fusion.6
  276.2 3.5 multiply_reduce_fusion.6
  286.5 3.3 fusion.183
  292.4 3.5 multiply_reduce_fusion.6
  323.7 4.7 all-to-all-start.3
  342.9 19.2 %collective-permute-done.25 = bf16[2,512,512]{2,1,0:T(8,128)(2,1)} collective-permute-done((bf16[2,512,512]{2,1,0:T(8,128)(2,1)}, bf16[2,512,512]{2,1,0:T(8,128)(2,1)}, u32[]{:S(2)}, u32[]{:S(2)}) %collective-permute-start.25) | collective-permute-done | bytes 1048608 | tf_op jit(solution)/shard_map/ppermute | solution.py:39
  364.6 5.4 %all-to-all-start.4 = ((bf16[8,2,64,512]{3,2,1,0:T(8,128)(2,1)}), bf16[8,2,64,512]{3,2,1,0:T(8,128)(2,1)}, u32[]{:S(2)}, u32[]{:S(2)}) async-start(bf16[8,2,64,512]{3,2,1,0:T(8,128)(2,1)} %copy.109), calls=%async_computation.4 | async-start | bytes 2097152 | tf_op jit(solution)/shard_map/all_to_all | solution.py:332
  383.2 6.4 %collective-permute-done.17 = bf16[4,64,128]{2,1,0:T(8,128)(2,1)S(1)} collective-permute-done((bf16[4,64,128]{2,1,0:T(8,128)(2,1)}, bf16[4,64,128]{2,1,0:T(8,128)(2,1)S(1)}, u32[]{:S(2)}, u32[]{:S(2)}) %collective-permute-start.17) | collective-permute-done | bytes 65568 | tf_op jit(solution)/shard_map/ppermute | solution.py:39
  389.6 5.7 %collective-permute-start.20 = (bf16[4,64,128]{2,1,0:T(8,128)(2,1)}, bf16[4,64,128]{2,1,0:T(8,128)(2,1)}, u32[]{:S(2)}, u32[]{:S(2)}) collective-permute-start(bf16[4,64,128]{2,1,0:T(8,128)(2,1)} %slice_reduce_fusion), channel_id=1, source_target_pairs={{0,20},{4,16},{8,28},{12,24},{16,4},{20,0},{24,12},{28,8},{1,21},{... | collective-permute-start | bytes 196616 | tf_op jit(solution)/shard_map/ppermute | solution.py:39
  396.8 4.0 all-to-all-done.4
  414.1 6.4 %all-to-all-start.5 = ((f32[8,32,512]{2,1,0:T(8,128)}), f32[8,32,512]{2,1,0:T(8,128)}, u32[]{:S(2)}, u32[]{:S(2)}) async-start(f32[8,32,512]{2,1,0:T(8,128)} %bitcast.454), calls=%async_computation.5 | async-start | bytes 1048576 | tf_op jit(solution)/shard_map/all_to_all | solution.py:201
  437.0 15.6 %newton.2 = f32[64,512]{1,0:T(8,128)} custom-call(f32[512,512]{1,0:T(8,128)} %gram.2.square_ref, f32[64,512]{1,0:T(8,128)} %constant_dynamic-slice_fusion.rows_ref), custom_call_target="tpu_custom_call" | custom-call | tf_op jit(solution)/shard_map/newton/pallas_call | solution.py:101
  454.1 3.5 convert_element_type.275
  492.1 15.5 %newton.3 = f32[128,512]{1,0:T(8,128)} custom-call(f32[512,512]{1,0:T(8,128)} %pad_maximum_fusion.2.square_ref, f32[128,512]{1,0:T(8,128)} %bitcast.453), custom_call_target="tpu_custom_call" | custom-call | tf_op jit(solution)/shard_map/newton/pallas_call | solution.py:101
  509.4 3.5 fusion.84
  513.0 4.1 collective-permute-done.35
  (420 shorter events, 251.9 us)
Async XLA Ops:
  7.2 188.4 %all-gather.8.cloned.1.call-start = ((), (), s32[]{:S(2)}) async-start(), calls=%async_computation.7 | async-start | bytes 4325376 | tf_op jit(solution)/shard_map/all_gather | solution.py:243
  8.9 420.4 %all-gather.6.cloned.1.call-start = ((), (), s32[]{:S(2)}) async-start(), calls=%async_computation.6 | async-start | bytes 1179648 | tf_op jit(solution)/shard_map/all_gather | solution.py:246
  10.7 86.6 %collective-permute-start.3 = (bf16[80,512]{1,0:T(8,128)(2,1)S(1)}, bf16[80,512]{1,0:T(8,128)(2,1)S(1)}, u32[]{:S(2)}, u32[]{:S(2)}) collective-permute-start(bf16[80,512]{1,0:T(8,128)(2,1)S(1)} %fusion.102), channel_id=1, source_target_pairs={{0,0},{1,8},{2,16},{3,24},{4,4},{5,12},{6,20},{7,28},{8,1},{9,9},{... | collective-permute-start | bytes 245768 | tf_op jit(solution)/shard_map/ppermute | solution.py:170
  11.4 86.0 %collective-permute-start.4 = (bf16[80,512]{1,0:T(8,128)(2,1)S(1)}, bf16[80,512]{1,0:T(8,128)(2,1)S(1)}, u32[]{:S(2)}, u32[]{:S(2)}) collective-permute-start(bf16[80,512]{1,0:T(8,128)(2,1)S(1)} %fusion.102), channel_id=1, source_target_pairs={{0,4},{1,12},{2,20},{3,28},{4,0},{5,8},{6,16},{7,24},{8,5},{9,13},... | collective-permute-start | bytes 245768 | tf_op jit(solution)/shard_map/ppermute | solution.py:170
  14.4 83.0 %collective-permute-start.5 = (bf16[80,512]{1,0:T(8,128)(2,1)S(1)}, bf16[80,512]{1,0:T(8,128)(2,1)S(1)}, u32[]{:S(2)}, u32[]{:S(2)}) collective-permute-start(bf16[80,512]{1,0:T(8,128)(2,1)S(1)} %fusion.102), channel_id=1, source_target_pairs={{0,8},{1,0},{2,24},{3,16},{4,12},{5,4},{6,28},{7,20},{8,9},{9,1},{... | collective-permute-start | bytes 245768 | tf_op jit(solution)/shard_map/ppermute | solution.py:170
  18.4 79.1 %collective-permute-start.6 = (bf16[80,512]{1,0:T(8,128)(2,1)S(1)}, bf16[80,512]{1,0:T(8,128)(2,1)S(1)}, u32[]{:S(2)}, u32[]{:S(2)}) collective-permute-start(bf16[80,512]{1,0:T(8,128)(2,1)S(1)} %fusion.102), channel_id=1, source_target_pairs={{0,12},{1,4},{2,28},{3,20},{4,8},{5,0},{6,24},{7,16},{8,13},{9,5},... | collective-permute-start | bytes 245768 | tf_op jit(solution)/shard_map/ppermute | solution.py:170
  18.4 80.8 %collective-permute-start.7 = (bf16[80,512]{1,0:T(8,128)(2,1)S(1)}, bf16[80,512]{1,0:T(8,128)(2,1)S(1)}, u32[]{:S(2)}, u32[]{:S(2)}) collective-permute-start(bf16[80,512]{1,0:T(8,128)(2,1)S(1)} %fusion.102), channel_id=1, source_target_pairs={{0,16},{1,24},{2,0},{3,8},{4,20},{5,28},{6,4},{7,12},{8,17},{9,25}... | collective-permute-start | bytes 245768 | tf_op jit(solution)/shard_map/ppermute | solution.py:170
  97.5 24.4 %collective-permute-start.10 = (bf16[80,512]{1,0:T(8,128)(2,1)S(1)}, bf16[80,512]{1,0:T(8,128)(2,1)S(1)}, u32[]{:S(2)}, u32[]{:S(2)}) collective-permute-start(bf16[80,512]{1,0:T(8,128)(2,1)S(1)} %fusion.102), channel_id=1, source_target_pairs={{0,28},{1,20},{2,12},{3,4},{4,24},{5,16},{6,8},{7,0},{8,29},{9,21}... | collective-permute-start | bytes 245768 | tf_op jit(solution)/shard_map/ppermute | solution.py:170
  97.6 22.3 %collective-permute-start.1 = (bf16[3,256,512]{2,1,0:T(8,128)(2,1)S(1)}, bf16[3,256,512]{2,1,0:T(8,128)(2,1)S(1)}, u32[]{:S(2)}, u32[]{:S(2)}) collective-permute-start(bf16[3,256,512]{2,1,0:T(8,128)(2,1)S(1)} %copy-done.27), channel_id=1, source_target_pairs={{0,2},{1,3},{2,0},{3,1},{4,6},{5,7},{6,4},{7,5},{8,10},{9,11},{10,... | collective-permute-start | bytes 2359304 | tf_op jit(solution)/shard_map/ppermute | solution.py:39
  99.2 25.7 %collective-permute-start = (bf16[3,256,512]{2,1,0:T(8,128)(2,1)S(1)}, bf16[3,256,512]{2,1,0:T(8,128)(2,1)}, u32[]{:S(2)}, u32[]{:S(2)}) collective-permute-start(bf16[3,256,512]{2,1,0:T(8,128)(2,1)S(1)} %copy-done.27), channel_id=1, source_target_pairs={{0,1},{1,0},{2,3},{3,2},{4,5},{5,4},{6,7},{7,6},{8,9},{9,8},{10,11... | collective-permute-start | bytes 2359304 | tf_op jit(solution)/shard_map/ppermute | solution.py:39
  103.5 298.6 %collective-permute-start.23 = (f32[64,512]{1,0:T(8,128)}, f32[64,512]{1,0:T(8,128)}, u32[]{:S(2)}, u32[]{:S(2)}) collective-permute-start(f32[64,512]{1,0:T(8,128)} %get-tuple-element.187), channel_id=1, source_target_pairs={{0,2},{1,3},{2,0},{3,1},{4,6},{5,7},{6,4},{7,5},{8,10},{9,11},{10,... | collective-permute-start | bytes 393224 | tf_op jit(solution)/shard_map/ppermute | solution.py:39
  123.3 55.9 %collective-permute-start.11 = (bf16[128,512]{1,0:T(8,128)(2,1)}, bf16[128,512]{1,0:T(8,128)(2,1)}, u32[]{:S(2)}, u32[]{:S(2)}) collective-permute-start(bf16[128,512]{1,0:T(8,128)(2,1)} %bitcast.52), channel_id=1, source_target_pairs={{0,1},{1,0},{2,3},{3,2},{4,5},{5,4},{6,7},{7,6},{8,9},{9,8},{10,11... | collective-permute-start | bytes 393224 | tf_op jit(solution)/shard_map/ppermute | solution.py:39
  123.4 55.8 %collective-permute-start.12 = (bf16[128,512]{1,0:T(8,128)(2,1)}, bf16[128,512]{1,0:T(8,128)(2,1)}, u32[]{:S(2)}, u32[]{:S(2)}) collective-permute-start(bf16[128,512]{1,0:T(8,128)(2,1)} %bitcast.52), channel_id=1, source_target_pairs={{0,2},{1,3},{2,0},{3,1},{4,6},{5,7},{6,4},{7,5},{8,10},{9,11},{10,... | collective-permute-start | bytes 393224 | tf_op jit(solution)/shard_map/ppermute | solution.py:39
  124.9 54.3 %collective-permute-start.13 = (bf16[128,512]{1,0:T(8,128)(2,1)}, bf16[128,512]{1,0:T(8,128)(2,1)}, u32[]{:S(2)}, u32[]{:S(2)}) collective-permute-start(bf16[128,512]{1,0:T(8,128)(2,1)} %bitcast.52), channel_id=1, source_target_pairs={{0,3},{1,2},{2,1},{3,0},{4,7},{5,6},{6,5},{7,4},{8,11},{9,10},{10,... | collective-permute-start | bytes 393224 | tf_op jit(solution)/shard_map/ppermute | solution.py:39
  163.3 27.3 %all-to-all-start = ((bf16[4,3,256,128]{3,2,1,0:T(8,128)(2,1)}), bf16[4,3,256,128]{3,2,1,0:T(8,128)(2,1)}, u32[]{:S(2)}, u32[]{:S(2)}) async-start(bf16[4,3,256,128]{3,2,1,0:T(8,128)(2,1)} %copy.90), calls=%async_computation | async-start | bytes 1572864 | tf_op jit(solution)/shard_map/all_to_all | solution.py:288
  217.1 17.8 %all-to-all-start.2 = ((bf16[4,128,512]{2,1,0:T(8,128)(2,1)}), bf16[4,128,512]{2,1,0:T(8,128)(2,1)}, u32[]{:S(2)}, u32[]{:S(2)}) async-start(bf16[4,128,512]{2,1,0:T(8,128)(2,1)} %bitcast.470), calls=%async_computation.2 | async-start | bytes 1048576 | tf_op jit(solution)/shard_map/all_to_all | solution.py:373
  234.8 17.5 %all-to-all-start.1 = ((bf16[4,3,256,128]{3,2,1,0:T(8,128)(2,1)}), bf16[4,3,256,128]{3,2,1,0:T(8,128)(2,1)}, u32[]{:S(2)}, u32[]{:S(2)}) async-start(bf16[4,3,256,128]{3,2,1,0:T(8,128)(2,1)} %bitcast.450), calls=%async_computation.1 | async-start | bytes 1572864 | tf_op jit(solution)/shard_map/all_to_all | solution.py:319
  245.8 83.7 %collective-permute-start.24 = (bf16[2,2,512,512]{3,2,1,0:T(8,128)(2,1)}, bf16[2,2,512,512]{3,2,1,0:T(8,128)(2,1)}, u32[]{:S(2)}, u32[]{:S(2)}) collective-permute-start(bf16[2,2,512,512]{3,2,1,0:T(8,128)(2,1)} %fusion.68), channel_id=1, source_target_pairs={{0,1},{1,0},{2,3},{3,2},{4,5},{5,4},{6,7},{7,6},{8,9},{9,8},{10,11... | collective-permute-start | bytes 6291464 | tf_op jit(solution)/shard_map/ppermute | solution.py:39
  323.7 40.8 %all-to-all-start.3 = ((bf16[32,80,128]{2,1,0:T(8,128)(2,1)}), bf16[32,80,128]{2,1,0:T(8,128)(2,1)}, u32[]{:S(2)}, u32[]{:S(2)}) async-start(bf16[32,80,128]{2,1,0:T(8,128)(2,1)} %pad_maximum_fusion.3), calls=%async_computation.3 | async-start | bytes 1310720 | tf_op jit(solution)/shard_map/all_to_all | solution.py:413
  334.1 27.9 %collective-permute-start.25 = (bf16[2,512,512]{2,1,0:T(8,128)(2,1)}, bf16[2,512,512]{2,1,0:T(8,128)(2,1)}, u32[]{:S(2)}, u32[]{:S(2)}) collective-permute-start(bf16[2,512,512]{2,1,0:T(8,128)(2,1)} %dynamic-slice_bitcast_fusion.1), channel_id=1, source_target_pairs={{0,2},{1,3},{2,0},{3,1},{4,6},{5,7},{6,4},{7,5},{8,10},{9,11},{10,... | collective-permute-start | bytes 3145736 | tf_op jit(solution)/shard_map/ppermute | solution.py:39
  364.6 36.2 %all-to-all-start.4 = ((bf16[8,2,64,512]{3,2,1,0:T(8,128)(2,1)}), bf16[8,2,64,512]{3,2,1,0:T(8,128)(2,1)}, u32[]{:S(2)}, u32[]{:S(2)}) async-start(bf16[8,2,64,512]{3,2,1,0:T(8,128)(2,1)} %copy.109), calls=%async_computation.4 | async-start | bytes 2097152 | tf_op jit(solution)/shard_map/all_to_all | solution.py:332
  371.4 82.7 %collective-permute-start.14 = (bf16[2,3,256,512]{3,2,1,0:T(8,128)(2,1)}, bf16[2,3,256,512]{3,2,1,0:T(8,128)(2,1)}, u32[]{:S(2)}, u32[]{:S(2)}) collective-permute-start(bf16[2,3,256,512]{3,2,1,0:T(8,128)(2,1)} %pad_maximum_fusion.1), channel_id=1, source_target_pairs={{0,1},{1,0},{2,3},{3,2},{4,5},{5,4},{6,7},{7,6},{8,9},{9,8},{10,11... | collective-permute-start | bytes 4718600 | tf_op jit(solution)/shard_map/ppermute | solution.py:39
  375.3 14.3 %collective-permute-start.17 = (bf16[4,64,128]{2,1,0:T(8,128)(2,1)}, bf16[4,64,128]{2,1,0:T(8,128)(2,1)S(1)}, u32[]{:S(2)}, u32[]{:S(2)}) collective-permute-start(bf16[4,64,128]{2,1,0:T(8,128)(2,1)} %slice_reduce_fusion), channel_id=1, source_target_pairs={{0,8},{4,12},{8,0},{12,4},{16,24},{20,28},{24,16},{28,20},{1,9},{5... | collective-permute-start | bytes 196616 | tf_op jit(solution)/shard_map/ppermute | solution.py:39
  376.8 19.1 %collective-permute-start.18 = (bf16[4,64,128]{2,1,0:T(8,128)(2,1)}, bf16[4,64,128]{2,1,0:T(8,128)(2,1)S(1)}, u32[]{:S(2)}, u32[]{:S(2)}) collective-permute-start(bf16[4,64,128]{2,1,0:T(8,128)(2,1)} %slice_reduce_fusion), channel_id=1, source_target_pairs={{0,12},{4,8},{8,4},{12,0},{16,28},{20,24},{24,20},{28,16},{1,13},{... | collective-permute-start | bytes 196616 | tf_op jit(solution)/shard_map/ppermute | solution.py:39
  380.3 27.4 %collective-permute-start.19 = (bf16[4,64,128]{2,1,0:T(8,128)(2,1)}, bf16[4,64,128]{2,1,0:T(8,128)(2,1)}, u32[]{:S(2)}, u32[]{:S(2)}) collective-permute-start(bf16[4,64,128]{2,1,0:T(8,128)(2,1)} %slice_reduce_fusion), channel_id=1, source_target_pairs={{0,16},{4,20},{8,24},{12,28},{16,0},{20,4},{24,8},{28,12},{1,17},{... | collective-permute-start | bytes 196616 | tf_op jit(solution)/shard_map/ppermute | solution.py:39
  389.6 19.6 %collective-permute-start.20 = (bf16[4,64,128]{2,1,0:T(8,128)(2,1)}, bf16[4,64,128]{2,1,0:T(8,128)(2,1)}, u32[]{:S(2)}, u32[]{:S(2)}) collective-permute-start(bf16[4,64,128]{2,1,0:T(8,128)(2,1)} %slice_reduce_fusion), channel_id=1, source_target_pairs={{0,20},{4,16},{8,28},{12,24},{16,4},{20,0},{24,12},{28,8},{1,21},{... | collective-permute-start | bytes 196616 | tf_op jit(solution)/shard_map/ppermute | solution.py:39
  395.9 14.7 %collective-permute-start.21 = (bf16[4,64,128]{2,1,0:T(8,128)(2,1)}, bf16[4,64,128]{2,1,0:T(8,128)(2,1)}, u32[]{:S(2)}, u32[]{:S(2)}) collective-permute-start(bf16[4,64,128]{2,1,0:T(8,128)(2,1)} %slice_reduce_fusion), channel_id=1, source_target_pairs={{0,24},{4,28},{8,16},{12,20},{16,8},{20,12},{24,0},{28,4},{1,25},{... | collective-permute-start | bytes 196616 | tf_op jit(solution)/shard_map/ppermute | solution.py:39
  402.2 18.3 %collective-permute-start.22 = (bf16[4,64,128]{2,1,0:T(8,128)(2,1)}, bf16[4,64,128]{2,1,0:T(8,128)(2,1)}, u32[]{:S(2)}, u32[]{:S(2)}) collective-permute-start(bf16[4,64,128]{2,1,0:T(8,128)(2,1)} %slice_reduce_fusion), channel_id=1, source_target_pairs={{0,28},{4,24},{8,20},{12,16},{16,12},{20,8},{24,4},{28,0},{1,29},{... | collective-permute-start | bytes 196616 | tf_op jit(solution)/shard_map/ppermute | solution.py:39
  414.1 43.5 %all-to-all-start.5 = ((f32[8,32,512]{2,1,0:T(8,128)}), f32[8,32,512]{2,1,0:T(8,128)}, u32[]{:S(2)}, u32[]{:S(2)}) async-start(f32[8,32,512]{2,1,0:T(8,128)} %bitcast.454), calls=%async_computation.5 | async-start | bytes 1048576 | tf_op jit(solution)/shard_map/all_to_all | solution.py:201
  462.8 9.8 %collective-permute-start.28 = (f32[32,512]{1,0:T(8,128)}, f32[32,512]{1,0:T(8,128)S(1)}, u32[]{:S(2)}, u32[]{:S(2)}) collective-permute-start(f32[32,512]{1,0:T(8,128)} %reduce_sum.274), channel_id=1, source_target_pairs={{0,8},{4,12},{8,0},{12,4},{16,24},{20,28},{24,16},{28,20},{1,9},{5... | collective-permute-start | bytes 196616 | tf_op jit(solution)/shard_map/ppermute | solution.py:39
  467.2 10.3 %collective-permute-start.31 = (f32[32,512]{1,0:T(8,128)}, f32[32,512]{1,0:T(8,128)S(1)}, u32[]{:S(2)}, u32[]{:S(2)}) collective-permute-start(f32[32,512]{1,0:T(8,128)} %reduce_sum.274), channel_id=1, source_target_pairs={{0,20},{4,16},{8,28},{12,24},{16,4},{20,0},{24,12},{28,8},{1,21},{... | collective-permute-start | bytes 196616 | tf_op jit(solution)/shard_map/ppermute | solution.py:39
  487.0 22.4 %collective-permute-start.15 = (bf16[3,256,512]{2,1,0:T(8,128)(2,1)}, bf16[3,256,512]{2,1,0:T(8,128)(2,1)}, u32[]{:S(2)}, u32[]{:S(2)}) collective-permute-start(bf16[3,256,512]{2,1,0:T(8,128)(2,1)} %fusion.81), channel_id=1, source_target_pairs={{0,2},{1,3},{2,0},{3,1},{4,6},{5,7},{6,4},{7,5},{8,10},{9,11},{10,... | collective-permute-start | bytes 2359304 | tf_op jit(solution)/shard_map/ppermute | solution.py:39
  (75 other events, 936.3 us)
Sparse Core Ops, SparseCore 0:
  11.6 65.9 all-gather.7
  79.7 40.3 all-gather.5
